TPU v7x, 128 devices: a whole 4x4x4 slice. The times are simulated.
128 devices in a mesh: seq: 16 (over z, x), tensor: 8 (over y, core).
Axes of the slice: x: 4, y: 4, z: 4, core: 2. Of those that a mesh axis runs over, the one named last changes fastest.
Arguments:
- queries: bfloat16 [4096, 4096], P('seq', 'tensor'), may hold values from -20 to 20
- out_grad: bfloat16 [4096, 4096], P('seq', 'tensor'), may hold values from -6 to 6
- neighbours: bfloat16 [18432, 4096], P('seq', 'tensor'), may hold values from -6 to 6
- key_weight: bfloat16 [4096, 4096], P(None, 'tensor'), may hold values from -0.09375 to 0.09375
- value_weight: bfloat16 [4096, 4096], P(None, 'tensor'), may hold values from -0.09375 to 0.09375
- owner: int32 [64, 2], replicated, may hold values from 0 to 15, as said below
- slot: int32 [64, 2], replicated, may hold values from 0 to 8, as said below
- lengths: int32 [16, 9], replicated, may hold values from 8 to 128, as said below
Outputs:
- query_grad: bfloat16 [4096, 4096], P('seq', 'tensor')
- key_weight_grad: float32 [4096, 4096], P('seq', 'tensor')
- value_weight_grad: float32 [4096, 4096], P('seq', 'tensor')
- neighbour_grad: bfloat16 [18432, 4096], P('seq', 'tensor')
Inputs may be any that keep to these rules, and one draw needn't show every extreme that they name: Each (owner, slot) pair is named by exactly one block's neighbour; the slots named on one shard are 0 to its count of neighbours minus 1; a shard holds at most 9 neighbours, and at least half of the shards hold exactly 9. The 8 neighbours of the blocks of one seq index come at most 1 from one shard. `slot`: see owner. `lengths`: every encoder shard has some neighbour with all 128 rows valid.
All inputs are finite; a program needn't handle non-finite values.
Results may differ from a plain program's by a relative error of at most 0.02.
The roundings to bfloat16 on the way count: a program that leaves them out, or rounds other values in their place, can miss the bound.
Values may be sent and summed in bfloat16 or wider, within the bound.
No kernel may reach another device: no remote copies, remote signals or barrier semaphores. Data moves between devices by JAX's collectives and lax.ppermute only.
A program may use at most 128 MiB of HBM per device.

v0:
```python
import jax
import jax.numpy as jnp
from jax import lax
from jax.sharding import PartitionSpec as P

HEAD = 128
BLOCK = 64
NEIGHBOUR_TOKENS = 128
NEIGH = 2
PEER = 1


def routing(owner, slot, lengths, seq_count, position, slot_count):
    refs = owner.size // seq_count
    holder_table = owner.reshape(seq_count, refs)
    slot_table = slot.reshape(seq_count, refs)
    my_holder = lax.dynamic_index_in_dim(holder_table, position, 0, keepdims=False)
    my_slot = lax.dynamic_index_in_dim(slot_table, position, 0, keepdims=False)
    ref_order = jnp.arange(refs, dtype=jnp.int32)
    earlier = ref_order[None, :] < ref_order[:, None]
    my_rank = jnp.sum((my_holder[:, None] == my_holder[None, :]) & earlier, axis=1)
    my_block = my_holder * PEER + my_rank
    my_lengths = jnp.take(lengths.reshape(-1), my_holder * slot_count + my_slot)
    matches = holder_table == position
    ranks = jnp.cumsum(matches.astype(jnp.int32), axis=1) - 1
    picks = matches[:, :, None] & (
        ranks[:, :, None] == jnp.arange(PEER, dtype=jnp.int32)[None, None, :]
    )
    send_slot = jnp.sum(jnp.where(picks, slot_table[:, :, None], 0), axis=1).reshape(-1)
    send_valid = jnp.any(picks, axis=1).reshape(-1)
    block_order = jnp.arange(seq_count * PEER, dtype=jnp.int32)
    slot_hits = send_valid[:, None] & (
        send_slot[:, None] == jnp.arange(slot_count, dtype=jnp.int32)[None, :]
    )
    slot_block = jnp.sum(jnp.where(slot_hits, block_order[:, None], 0), axis=0)
    slot_live = jnp.any(slot_hits, axis=0)
    ref_hits = my_block[:, None] == block_order[None, :]
    block_ref = jnp.sum(jnp.where(ref_hits, ref_order[:, None], 0), axis=0)
    block_live = jnp.any(ref_hits, axis=0)
    return (
        my_block,
        my_lengths,
        send_slot,
        send_valid,
        slot_block,
        slot_live,
        block_ref,
        block_live,
    )


def select_blocks(source, index, live):
    taken = jnp.take(source, index, axis=0)
    return jnp.where(live[:, None, None], taken, jnp.zeros((), source.dtype))


def attend_back(queries, out_grad, key_rows, value_rows, valid_lengths):
    tokens, width = queries.shape
    blocks = tokens // BLOCK
    heads = width // HEAD
    span = NEIGH * NEIGHBOUR_TOKENS
    scale = HEAD ** (-0.5)
    query_heads = queries.reshape(blocks, BLOCK, heads, HEAD)
    grad_heads = out_grad.reshape(blocks, BLOCK, heads, HEAD)
    key_heads = key_rows.reshape(blocks, span, heads, HEAD)
    value_heads = value_rows.reshape(blocks, span, heads, HEAD)
    valid_keys = (
        jnp.arange(NEIGHBOUR_TOKENS, dtype=jnp.int32)[None, :] < valid_lengths[:, None]
    ).reshape(blocks, span)
    scores = (
        jnp.einsum("cqhd,ckhd->chqk", query_heads, key_heads, preferred_element_type=jnp.float32)
        * scale
    )
    scores = jnp.where(valid_keys[:, None, None, :], scores, -jnp.inf)
    highest = jnp.max(scores, axis=-1, keepdims=True)
    raised = jnp.exp(scores - highest)
    attention = raised / jnp.sum(raised, axis=-1, keepdims=True)
    attention_low = attention.astype(jnp.bfloat16)
    attended = jnp.einsum(
        "chqk,ckhd->cqhd", attention_low, value_heads, preferred_element_type=jnp.float32
    )
    delta = jnp.sum(attended * grad_heads.astype(jnp.float32), axis=-1).transpose(0, 2, 1)[
        ..., None
    ]
    value_grad = jnp.einsum(
        "chqk,cqhd->ckhd", attention_low, grad_heads, preferred_element_type=jnp.float32
    ).astype(jnp.bfloat16)
    prob_grad = jnp.einsum(
        "cqhd,ckhd->chqk", grad_heads, value_heads, preferred_element_type=jnp.float32
    )
    score_grad = (attention * (prob_grad - delta) * scale).astype(jnp.bfloat16)
    query_grad = jnp.einsum(
        "chqk,ckhd->cqhd", score_grad, key_heads, preferred_element_type=jnp.float32
    ).astype(jnp.bfloat16)
    key_grad = jnp.einsum(
        "chqk,cqhd->ckhd", score_grad, query_heads, preferred_element_type=jnp.float32
    ).astype(jnp.bfloat16)
    refs = blocks * NEIGH
    pair_grads = jnp.concatenate(
        [
            key_grad.reshape(refs, NEIGHBOUR_TOKENS, width),
            value_grad.reshape(refs, NEIGHBOUR_TOKENS, width),
        ],
        axis=-1,
    )
    return (query_grad.reshape(tokens, width), pair_grads)


def weight_term(rows_here, grads_here):
    return lax.dot_general(
        rows_here, grads_here, (((0,), (0,)), ((), ())), preferred_element_type=jnp.float32
    )


def input_term(grads_here, key_weight, value_weight):
    width = key_weight.shape[1]
    dims = (((1,), (1,)), ((), ()))
    term = lax.dot_general(
        grads_here[:, :width], key_weight, dims, preferred_element_type=jnp.float32
    )
    return term + lax.dot_general(
        grads_here[:, width:], value_weight, dims, preferred_element_type=jnp.float32
    )


def project(rows_here, key_weight, value_weight):
    key_rows = jnp.dot(rows_here, key_weight, preferred_element_type=jnp.float32).astype(
        jnp.bfloat16
    )
    value_rows = jnp.dot(rows_here, value_weight, preferred_element_type=jnp.float32).astype(
        jnp.bfloat16
    )
    return (key_rows, value_rows)


def local(queries, out_grad, neighbours, key_weight, value_weight, owner, slot, lengths):
    seq_count = lax.axis_size("seq")
    position = lax.axis_index("seq")
    slot_count = lengths.shape[1]
    width = key_weight.shape[1]
    my_block, my_lengths, send_slot, send_valid, slot_block, slot_live, block_ref, block_live = (
        routing(owner, slot, lengths, seq_count, position, slot_count)
    )
    gathered = lax.all_gather(neighbours, "tensor", axis=1, tiled=True)
    key_rows, value_rows = project(gathered, key_weight, value_weight)
    packed = jnp.concatenate([key_rows, value_rows], axis=1).reshape(
        slot_count, NEIGHBOUR_TOKENS, 2 * width
    )
    outgoing = select_blocks(packed, send_slot, send_valid)
    incoming = lax.all_to_all(outgoing, "seq", split_axis=0, concat_axis=0, tiled=True)
    reading = jnp.take(incoming, my_block, axis=0)
    query_grad, pair_grads = attend_back(
        queries, out_grad, reading[:, :, :width], reading[:, :, width:], my_lengths
    )
    returning = select_blocks(pair_grads, block_ref, block_live)
    arrived = lax.all_to_all(returning, "seq", split_axis=0, concat_axis=0, tiled=True)
    slot_grads = select_blocks(arrived, slot_block, slot_live).reshape(
        slot_count * NEIGHBOUR_TOKENS, 2 * width
    )
    weight_grads = lax.psum_scatter(
        weight_term(gathered, slot_grads).astype(jnp.bfloat16),
        "seq",
        scatter_dimension=0,
        tiled=True,
    ).astype(jnp.float32)
    feature_part = input_term(slot_grads, key_weight, value_weight)
    neighbour_grad = lax.psum_scatter(
        feature_part.astype(jnp.bfloat16), "tensor", scatter_dimension=1, tiled=True
    )
    return (query_grad, weight_grads[:, :width], weight_grads[:, width:], neighbour_grad)


def solution(mesh):
    placed = (
        P("seq", "tensor"),
        P("seq", "tensor"),
        P("seq", "tensor"),
        P(None, "tensor"),
        P(None, "tensor"),
        P(),
        P(),
        P(),
    )
    return jax.shard_map(
        local,
        mesh=mesh,
        in_specs=placed,
        out_specs=(P("seq", "tensor"), P("seq", "tensor"), P("seq", "tensor"), P("seq", "tensor")),
        check_vma=False,
    )
```

profile of v0, /device:TPU:6, one launch (start us, length us, event | category | flops | bytes accessed | tf_op | source)
XLA Modules:
  0.0 433.6 jit_solution(3052797613657873586)
XLA Ops:
  12.1 54.0 %all-gather.2.cloned.1.call-done = bf16[1152,4096]{1,0:T(8,128)(2,1)} async-done(((bf16[1152,512]{1,0:T(8,128)(2,1)}), bf16[1152,4096]{1,0:T(8,128)(2,1)}) %all-gather.2.cloned.1.call-update) | async-done | bytes 9437200 | tf_op jit(solution)/shard_map/all_gather | solution.py:144
  66.1 10.5 %convolution_convert_fusion = bf16[1152,512]{0,1:T(8,128)(2,1)S(1)} fusion(bf16[1152,4096]{1,0:T(8,128)(2,1)} %all-gather.2.cloned.1.call-done, bf16[4096,512]{1,0:T(8,128)(2,1)} %param.12), kind=kOutput, calls=%fused_computation.10 | convolution fusion | flops 4832428032 | bytes 14811136 | tf_op jit(solution)/shard_map/dot_general | solution.py:130
  76.7 6.1 %convolution_convert_fusion.1 = bf16[1152,512]{0,1:T(8,128)(2,1)S(1)} fusion(bf16[1152,4096]{1,0:T(8,128)(2,1)S(1)} %copy-done.7, bf16[4096,512]{1,0:T(8,128)(2,1)S(1)} %copy-done.8), kind=kOutput, calls=%fused_computation.11 | convolution fusion | flops 4832428032 | bytes 14811136 | tf_op jit(solution)/shard_map/dot_general | solution.py:127
  82.8 1.6 pad_maximum_fusion
  84.4 2.8 copy.63
  87.2 2.8 gather_fusion
  90.0 4.7 %select_select_fusion.1 = bf16[16,128,1024]{2,1,0:T(8,128)(2,1)} fusion(bf16[16,128,1024]{2,1,0:T(8,128)(2,1)} %gather_fusion, pred[16]{0:T(512)(128)(4,1)S(1)} %get-tuple-element.35, pred[16]{0:T(512)(128)(4,1)S(1)} %reduce_or.36), kind=kLoop, calls=%fused_computation.9 | loop fusion | flops 4194304 | bytes 8388640 | tf_op jit(solution)/shard_map/jit(_where)/select_n | solution.py:54
  94.7 7.5 %all-to-all-start = ((bf16[16,128,1024]{2,1,0:T(8,128)(2,1)}), bf16[16,128,1024]{2,1,0:T(8,128)(2,1)}, u32[]{:S(2)}, u32[]{:S(2)}) async-start(bf16[16,128,1024]{2,1,0:T(8,128)(2,1)} %select_select_fusion.1), calls=%async_computation | async-start | bytes 8388608 | tf_op jit(solution)/shard_map/all_to_all | solution.py:150
  104.2 59.8 %all-to-all-done = bf16[16,128,1024]{2,1,0:T(8,128)(2,1)} async-done(((bf16[16,128,1024]{2,1,0:T(8,128)(2,1)}), bf16[16,128,1024]{2,1,0:T(8,128)(2,1)}, u32[]{:S(2)}, u32[]{:S(2)}) %all-to-all-start) | async-done | bytes 4194336 | tf_op jit(solution)/shard_map/all_to_all | solution.py:150
  164.0 2.9 gather_fusion.1
  168.5 1.2 fusion.42
  169.7 4.2 fusion.4
  173.9 2.9 fusion.16
  176.8 2.0 copy.76
  178.9 1.2 reshape.245
  180.1 1.8 fusion.11
  184.0 1.2 reshape.244
  185.2 1.8 pad_maximum_fusion.1
  187.1 2.8 gather_fusion.3
  189.8 4.7 %select_select_fusion = bf16[16,128,1024]{2,1,0:T(8,128)(2,1)} fusion(bf16[16,128,1024]{2,1,0:T(8,128)(2,1)} %gather_fusion.3, pred[16]{0:T(512)(128)(4,1)S(1)} %get-tuple-element.34, pred[16]{0:T(512)(128)(4,1)S(1)} %fusion.29), kind=kLoop, calls=%fused_computation.8 | loop fusion | flops 4194304 | bytes 8388640 | tf_op jit(solution)/shard_map/jit(_where)/select_n | solution.py:54
  194.5 7.0 %all-to-all-start.1 = ((bf16[16,128,1024]{2,1,0:T(8,128)(2,1)}), bf16[16,128,1024]{2,1,0:T(8,128)(2,1)}, u32[]{:S(2)}, u32[]{:S(2)}) async-start(bf16[16,128,1024]{2,1,0:T(8,128)(2,1)} %select_select_fusion), calls=%async_computation.1 | async-start | bytes 8388608 | tf_op jit(solution)/shard_map/all_to_all | solution.py:156
  201.8 58.8 %all-to-all-done.1 = bf16[16,128,1024]{2,1,0:T(8,128)(2,1)} async-done(((bf16[16,128,1024]{2,1,0:T(8,128)(2,1)}), bf16[16,128,1024]{2,1,0:T(8,128)(2,1)}, u32[]{:S(2)}, u32[]{:S(2)}) %all-to-all-start.1) | async-done | bytes 4194336 | tf_op jit(solution)/shard_map/all_to_all | solution.py:156
  260.6 2.9 gather_fusion.4
  264.4 1.4 copy-done
  265.8 16.8 %convert_bitcast_fusion = bf16[4096,1024]{0,1:T(8,128)(2,1)} fusion(bf16[1152,1024]{1,0:T(8,128)(2,1)S(1)} %fusion.1, bf16[1152,4096]{1,0:T(8,128)(2,1)} %all-gather.2.cloned.1.call-done), kind=kOutput, calls=%fused_computation.7 | convolution fusion | flops 9667870720 | bytes 20185088 | tf_op jit(solution)/shard_map/dot_general | solution.py:110
  282.9 1.4 copy-done.1
  284.3 11.5 %fusion.14 = f32[1152,4096]{1,0:T(8,128)} fusion(bf16[4096,512]{1,0:T(8,128)(2,1)} %param.11, bf16[1152,1024]{1,0:T(8,128)(2,1)S(1)} %copy-done.1), kind=kOutput, calls=%fused_computation.35 | convolution fusion | flops 4831838208 | bytes 24248320 | tf_op jit(solution)/shard_map/dot_general | solution.py:118
  295.8 11.6 %add_convert_fusion = bf16[1152,4096]{1,0:T(8,128)(2,1)} fusion(f32[1152,4096]{1,0:T(8,128)} %fusion.14, bf16[4096,512]{1,0:T(8,128)(2,1)S(1)} %copy-done.9, bf16[1152,1024]{1,0:T(8,128)(2,1)S(1)} %copy-done.1), kind=kOutput, calls=%fused_computation.6 | convolution fusion | flops 4841275392 | bytes 33685504 | tf_op jit(solution)/shard_map/dot_general | solution.py:121
  307.4 1.0 copy-done.3
  309.7 57.7 %reduce-scatter.3.cloned.1.call-done = bf16[256,1024]{0,1:T(8,128)(2,1)} async-done(((bf16[4096,1024]{0,1:T(8,128)(2,1)}), bf16[256,1024]{0,1:T(8,128)(2,1)}) %reduce-scatter.3.cloned.1.call-update) | async-done | bytes 524304 | tf_op jit(solution)/shard_map/reduce_scatter | solution.py:160
  367.4 1.1 fusion.41
  370.5 56.6 %reduce-scatter.5.cloned.1.call-done = bf16[1152,512]{1,0:T(8,128)(2,1)} async-done(((bf16[1152,4096]{1,0:T(8,128)(2,1)}), bf16[1152,512]{1,0:T(8,128)(2,1)}) %reduce-scatter.5.cloned.1.call-update) | async-done | bytes 1179664 | tf_op jit(solution)/shard_map/reduce_scatter | solution.py:167
  (79 shorter events, 15.3 us)
Async XLA Ops:
  7.2 59.0 %all-gather.2.cloned.1.call-start = ((), (), s32[]{:S(2)}) async-start(), calls=%async_computation.4 | async-start | bytes 10616832 | tf_op jit(solution)/shard_map/all_gather | solution.py:144
  66.1 10.5 %copy-start.7 = (bf16[1152,4096]{1,0:T(8,128)(2,1)S(1)}, bf16[1152,4096]{1,0:T(8,128)(2,1)}, u32[]{:S(2)}) copy-start(bf16[1152,4096]{1,0:T(8,128)(2,1)} %all-gather.2.cloned.1.call-done) | copy-start | bytes 28311556
  66.1 10.5 %copy-start.8 = (bf16[4096,512]{1,0:T(8,128)(2,1)S(1)}, bf16[4096,512]{1,0:T(8,128)(2,1)}, u32[]{:S(2)}) copy-start(bf16[4096,512]{1,0:T(8,128)(2,1)} %param.11) | copy-start | bytes 12582916
  94.7 7.5 %copy-start.6 = (s32[16,9]{1,0:T(8,128)S(1)}, s32[16,9]{1,0:T(8,128)}, u32[]{:S(2)}) copy-start(s32[16,9]{1,0:T(8,128)} %param.15) | copy-start | bytes 1732
  94.7 8.5 %copy-start.4 = (bf16[256,512]{1,0:T(8,128)(2,1)S(1)}, bf16[256,512]{1,0:T(8,128)(2,1)}, u32[]{:S(2)}) copy-start(bf16[256,512]{1,0:T(8,128)(2,1)} %param.9) | copy-start | bytes 786436
  94.7 9.2 %copy-start.5 = (bf16[256,512]{1,0:T(8,128)(2,1)S(1)}, bf16[256,512]{1,0:T(8,128)(2,1)}, u32[]{:S(2)}) copy-start(bf16[256,512]{1,0:T(8,128)(2,1)} %param.8) | copy-start | bytes 786436
  94.7 69.4 %all-to-all-start = ((bf16[16,128,1024]{2,1,0:T(8,128)(2,1)}), bf16[16,128,1024]{2,1,0:T(8,128)(2,1)}, u32[]{:S(2)}, u32[]{:S(2)}) async-start(bf16[16,128,1024]{2,1,0:T(8,128)(2,1)} %select_select_fusion.1), calls=%async_computation | async-start | bytes 8388608 | tf_op jit(solution)/shard_map/all_to_all | solution.py:150
  181.9 0.8 copy-start.2
  194.5 66.2 %all-to-all-start.1 = ((bf16[16,128,1024]{2,1,0:T(8,128)(2,1)}), bf16[16,128,1024]{2,1,0:T(8,128)(2,1)}, u32[]{:S(2)}, u32[]{:S(2)}) async-start(bf16[16,128,1024]{2,1,0:T(8,128)(2,1)} %select_select_fusion), calls=%async_computation.1 | async-start | bytes 8388608 | tf_op jit(solution)/shard_map/all_to_all | solution.py:156
  201.5 165.9 %reduce-scatter.3.cloned.1.call-start = ((), (), s32[]{:S(2)}) async-start(), calls=%async_computation.5 | async-start | bytes 8912896 | tf_op jit(solution)/shard_map/reduce_scatter | solution.py:160
  264.4 1.4 copy-start
  282.6 1.7 copy-start.1
  282.7 144.4 %reduce-scatter.5.cloned.1.call-start = ((), (), s32[]{:S(2)}) async-start(), calls=%async_computation.6 | async-start | bytes 10616832 | tf_op jit(solution)/shard_map/reduce_scatter | solution.py:167
  284.3 11.5 %copy-start.9 = (bf16[4096,512]{1,0:T(8,128)(2,1)S(1)}, bf16[4096,512]{1,0:T(8,128)(2,1)}, u32[]{:S(2)}) copy-start(bf16[4096,512]{1,0:T(8,128)(2,1)} %param.12) | copy-start | bytes 12582916
  307.4 1.1 copy-start.3
Sparse Core Ops, SparseCore 0:
  9.7 56.3 all-gather.1
  282.8 84.5 reduce-scatter.2
  370.4 56.6 reduce-scatter.4
where the time goes:
time: 435 us; the launch traced here: 434 us
  waiting for transfers between devices  288 us (66%)
  matrix products  66.7 us (15%)
  local copies, waits for them, and re-layouts  32.8 us (8%)
  other arithmetic  17.6 us (4%)
  starting transfers between devices  14.9 us (3%)
  between operations  14 us (3%)
    all_to_all x1, waiting for transfers between devices, local(): lax.all_to_all(outgoing, 'seq', split_axis=0, concat_axis=0, tiled=True)  59.8 us
    all_to_all x1, waiting for transfers between devices, local(): lax.all_to_all(returning, 'seq', split_axis=0, concat_axis=0, tiled=True)  58.8 us
    reduce_scatter x1, waiting for transfers between devices, local(): lax.psum_scatter(weight_term(gathered, slot_grads).astype(jnp.bfloat16),...  57.7 us
    reduce_scatter x1, waiting for transfers between devices, local(): lax.psum_scatter(feature_part.astype(jnp.bfloat16), 'tensor', scatter_dim...  56.6 us
    all_gather x1, waiting for transfers between devices, local(): gathered = lax.all_gather(neighbours, 'tensor', axis=1, tiled=True)  54 us
    dot_general x1, matrix products, weight_term(): lax.dot_general(rows_here, grads_here, (((0,), (0,)), ((), ())), preferre...  16.8 us
    dot_general x1, matrix products, input_term(): lax.dot_general(grads_here[:, width:], value_weight, dims, preferred_elem...  11.6 us
    dot_general x1, matrix products, input_term(): lax.dot_general(grads_here[:, :width], key_weight, dims, preferred_elemen...  11.5 us
  transfers between devices with their start and end apart: 5, of which 5 were waited for; matrix products, arithmetic and copies ran while one was open for 8% of the time, Pallas kernels for 0%

commit v1 on v0

v1 whole, which is shorter than its diff:
```python
import jax
import jax.numpy as jnp
from jax import lax
from jax.experimental import pallas as pl
from jax.experimental.pallas import tpu as pltpu
from jax.sharding import PartitionSpec as P

HEAD = 128
BLOCK = 64
NT = 128
NEIGH = 2
VMEM_LIMIT = 48 * 1024 * 1024
F32 = jnp.float32
BF16 = jnp.bfloat16


def params():
    return pltpu.CompilerParams(vmem_limit_bytes=VMEM_LIMIT)


def cost(flops, moved):
    return pl.CostEstimate(flops=flops, bytes_accessed=moved, transcendentals=0)


def dot(a, b, ca, cb):
    return lax.dot_general(a, b, (((ca,), (cb,)), ((), ())), preferred_element_type=F32)


def project(rows, key_weight, value_weight):
    parts, count, depth = rows.shape
    width = key_weight.shape[1]

    def body(r_ref, k_ref, v_ref, o_ref, acc):
        step = pl.program_id(0)

        @pl.when(step == 0)
        def _():
            acc[...] = jnp.zeros_like(acc)

        acc[:, :width] += dot(r_ref[0], k_ref[...], 1, 0)
        acc[:, width:] += dot(r_ref[0], v_ref[...], 1, 0)

        @pl.when(step == parts - 1)
        def _():
            o_ref[...] = acc[...].astype(BF16)

    return pl.pallas_call(
        body,
        grid=(parts,),
        in_specs=[
            pl.BlockSpec((1, count, depth), lambda i: (i, 0, 0)),
            pl.BlockSpec((depth, width), lambda i: (i, 0)),
            pl.BlockSpec((depth, width), lambda i: (i, 0)),
        ],
        out_specs=pl.BlockSpec((count, 2 * width), lambda i: (0, 0)),
        out_shape=jax.ShapeDtypeStruct((count, 2 * width), BF16),
        scratch_shapes=[pltpu.VMEM((count, 2 * width), F32)],
        compiler_params=params(),
        cost_estimate=cost(4 * parts * count * depth * width, 20 << 20),
        name="project",
    )(rows, key_weight, value_weight)


def attend_back(queries, out_grad, pair_rows, lengths):
    tokens, width = queries.shape
    blocks = tokens // BLOCK
    heads = width // HEAD
    span = NEIGH * NT
    scale = HEAD ** (-0.5)

    def body(len_ref, q_ref, g_ref, kv_ref, dq_ref, p_ref, t_ref):
        block = pl.program_id(0)
        column = lax.broadcasted_iota(jnp.int32, (BLOCK, span), 1)
        first = len_ref[block * NEIGH]
        second = len_ref[block * NEIGH + 1]
        valid = (column < first) | ((column >= NT) & (column < NT + second))
        for h in range(heads):
            cols = slice(h * HEAD, (h + 1) * HEAD)
            vcols = slice(width + h * HEAD, width + (h + 1) * HEAD)
            q = q_ref[:, cols]
            g = g_ref[:, cols]
            k = kv_ref[:, cols]
            v = kv_ref[:, vcols]
            scores = jnp.where(valid, dot(q, k, 1, 1) * scale, -jnp.inf)
            raised = jnp.exp(scores - jnp.max(scores, axis=1, keepdims=True))
            attention = raised / jnp.sum(raised, axis=1, keepdims=True)
            low = attention.astype(BF16)
            prob_grad = dot(g, v, 1, 1)
            delta = jnp.sum(low.astype(F32) * prob_grad, axis=1, keepdims=True)
            score_grad = (attention * (prob_grad - delta) * scale).astype(BF16)
            dq_ref[:, cols] = dot(score_grad, k, 1, 0).astype(BF16)
            p_ref[:, cols] = dot(score_grad, q, 0, 0).astype(BF16)
            p_ref[:, vcols] = dot(low, g, 0, 0).astype(BF16)
            t_ref[cols, :] = dot(q, score_grad, 0, 0).astype(BF16)
            t_ref[vcols, :] = dot(g, low, 0, 0).astype(BF16)

    count = blocks * span
    return pl.pallas_call(
        body,
        grid_spec=pltpu.PrefetchScalarGridSpec(
            num_scalar_prefetch=1,
            grid=(blocks,),
            in_specs=[
                pl.BlockSpec((BLOCK, width), lambda i, n: (i, 0)),
                pl.BlockSpec((BLOCK, width), lambda i, n: (i, 0)),
                pl.BlockSpec((span, 2 * width), lambda i, n: (i, 0)),
            ],
            out_specs=[
                pl.BlockSpec((BLOCK, width), lambda i, n: (i, 0)),
                pl.BlockSpec((span, 2 * width), lambda i, n: (i, 0)),
                pl.BlockSpec((2 * width, span), lambda i, n: (0, i)),
            ],
        ),
        out_shape=[
            jax.ShapeDtypeStruct((tokens, width), BF16),
            jax.ShapeDtypeStruct((count, 2 * width), BF16),
            jax.ShapeDtypeStruct((2 * width, count), BF16),
        ],
        compiler_params=params(),
        cost_estimate=cost(7 * 2 * tokens * span * width, 8 << 20),
        name="attend_back",
    )(lengths, queries, out_grad, pair_rows)


def weight_groups(grads_t, rows, groups, split):
    width, count = grads_t.shape[0] // 2, grads_t.shape[1]
    chunk = 256
    total = len(groups) * split
    halves = [g[0] for g in groups]
    ids = jnp.stack([jnp.stack(g[1] + g[2]) for g in groups]).reshape(-1).astype(jnp.int32)

    def body(id_ref, *refs):
        t_refs, r_refs, o_refs = refs[:2], refs[2 : 2 + len(groups)], refs[2 + len(groups) :]
        for half, r_ref, o_ref in zip(halves, r_refs, o_refs):
            o_ref[0] = dot(t_refs[half][...], r_ref[0], 1, 0).astype(BF16)

    def row_spec(n):
        base = n * 2 * split
        return pl.BlockSpec((1, count, chunk), lambda i, s: (s[base + i], 0, s[base + split + i]))

    return pl.pallas_call(
        body,
        grid_spec=pltpu.PrefetchScalarGridSpec(
            num_scalar_prefetch=1,
            grid=(split,),
            in_specs=[
                pl.BlockSpec((width, count), lambda i, s: (0, 0)),
                pl.BlockSpec((width, count), lambda i, s: (1, 0)),
            ]
            + [row_spec(n) for n in range(len(groups))],
            out_specs=[pl.BlockSpec((1, width, chunk), lambda i, s: (i, 0, 0)) for _ in groups],
        ),
        out_shape=[jax.ShapeDtypeStruct((split, width, chunk), BF16) for _ in groups],
        compiler_params=params(),
        cost_estimate=cost(2 * total * width * count * chunk, total * 3 << 18),
        name="weight_groups",
    )(ids, grads_t, grads_t, *([rows] * len(groups)))


def row_part(pair, key_weight, value_weight):
    count = pair.shape[0]
    features, width = key_weight.shape
    tile = 512

    def body(p_ref, k_ref, v_ref, o_ref):
        term = dot(p_ref[:, :width], k_ref[...], 1, 1)
        o_ref[...] = (term + dot(p_ref[:, width:], v_ref[...], 1, 1)).astype(BF16)

    return pl.pallas_call(
        body,
        grid=(features // tile,),
        in_specs=[
            pl.BlockSpec((count, 2 * width), lambda i: (0, 0)),
            pl.BlockSpec((tile, width), lambda i: (i, 0)),
            pl.BlockSpec((tile, width), lambda i: (i, 0)),
        ],
        out_specs=pl.BlockSpec((count, tile), lambda i: (0, i)),
        out_shape=jax.ShapeDtypeStruct((count, features), BF16),
        compiler_params=params(),
        cost_estimate=cost(4 * count * features * width, 18 << 20),
        name="row_part",
    )(pair, key_weight, value_weight)


def shift(value, axis, step):
    def moved(i):
        z, x = i // 4, i % 4
        return ((z + step) % 4) * 4 + x if axis == "z" else z * 4 + (x + step) % 4

    return lax.ppermute(value, "seq", [(i, moved(i)) for i in range(16)])


def add(*terms):
    total = terms[0].astype(F32)
    for term in terms[1:]:
        total = total + term.astype(F32)
    return total.astype(BF16)


def ring_first(axis, far_lo, far_hi, next_lo, next_hi, last_lo, last_hi):
    via_up = shift(far_lo, axis, 1)
    via_down = shift(far_hi, axis, -1)
    up_hi = shift(next_hi, axis, 1)
    down_lo = shift(last_lo, axis, -1)
    up_lo = shift(add(next_lo, via_up), axis, 1)
    down_hi = shift(add(last_hi, via_down), axis, -1)
    return (up_lo, down_lo), (up_hi, down_hi)


def weight_grads(grads_t, rows):
    spot = lax.axis_index("seq")
    z, x = spot // 4, spot % 4

    def key_group(step, pick):
        col = (x + step) % 4
        return (0, [2 * ((z + d) % 4) + col // 2 for d in pick], [col % 2 for _ in pick])

    def value_group(step, pick):
        return (
            1,
            [2 * ((z + step) % 4) + ((x + d) % 4) // 2 for d in pick],
            [((x + d) % 4) % 2 for d in pick],
        )

    lo, hi = (0, 1), (2, 3)
    k2l, k2h, v2l, v2h = weight_groups(
        grads_t, rows, [key_group(2, lo), key_group(2, hi), value_group(2, lo), value_group(2, hi)], 2
    )
    k1l, k1h, k3l, k3h, v1l, v1h, v3l, v3h = weight_groups(
        grads_t,
        rows,
        [
            key_group(1, lo), key_group(1, hi), key_group(3, lo), key_group(3, hi),
            value_group(1, lo), value_group(1, hi), value_group(3, lo), value_group(3, hi),
        ],
        2,
    )
    own = weight_groups(
        grads_t, rows, [key_group(0, lo), key_group(0, hi), value_group(0, lo), value_group(0, hi)], 2
    )
    key_lo, key_hi = ring_first("x", k2l, k2h, k1l, k1h, k3l, k3h)
    value_lo, value_hi = ring_first("z", v2l, v2h, v1l, v1h, v3l, v3h)
    done = []
    for axis, o_lo, o_hi, (a, b), (c, d) in (
        ("z", own[0], own[1], key_lo, key_hi),
        ("x", own[2], own[3], value_lo, value_hi),
    ):
        half = o_lo.shape[1] // 2
        far = add(o_hi[0], c[0], d[0])
        after = add(o_lo[1], a[1], b[1])
        before = add(o_hi[1], c[1], d[1])
        via_up = shift(far[:half], axis, 1)
        via_down = shift(far[half:], axis, -1)
        up_hi = shift(after[half:], axis, 1)
        down_lo = shift(before[:half], axis, -1)
        up_lo = shift(add(after[:half], via_up), axis, 1)
        down_hi = shift(add(before[half:], via_down), axis, -1)
        mine = o_lo[0].astype(F32) + a[0].astype(F32) + b[0].astype(F32)
        low = mine[:half] + up_lo.astype(F32) + down_lo.astype(F32)
        high = mine[half:] + up_hi.astype(F32) + down_hi.astype(F32)
        done.append(jnp.concatenate([low, high], axis=0).T)
    return done


def local(queries, out_grad, neighbours, key_weight, value_weight, owner, slot, lengths):
    seq_count = lax.axis_size("seq")
    position = lax.axis_index("seq")
    slot_count = lengths.shape[1]
    width = key_weight.shape[1]
    holders = owner.reshape(seq_count, -1)
    slots = slot.reshape(seq_count, -1)
    refs = holders.shape[1]
    order = jnp.arange(refs, dtype=jnp.int32)
    readers = jnp.arange(seq_count, dtype=jnp.int32)

    mine = holders == position
    send_slot = jnp.sum(jnp.where(mine, slots, 0), axis=1)
    my_holder = lax.dynamic_index_in_dim(holders, position, 0, keepdims=False)
    my_slot = lax.dynamic_index_in_dim(slots, position, 0, keepdims=False)
    my_lengths = jnp.take(lengths.reshape(-1), my_holder * slot_count + my_slot, mode="clip")
    back_ref = jnp.sum(jnp.where(my_holder[:, None] == readers[None, :], order[:, None], 0), axis=0)
    reads = mine[:, :, None] & (slots[:, :, None] == jnp.arange(slot_count, dtype=jnp.int32))
    slot_reader = jnp.sum(jnp.where(reads, readers[:, None, None], 0), axis=(0, 1))
    slot_live = jnp.any(reads, axis=(0, 1))

    outgoing = jnp.take(neighbours.reshape(slot_count, NT, width), send_slot, axis=0, mode="clip")
    incoming = lax.all_to_all(outgoing, "seq", split_axis=0, concat_axis=0, tiled=True)
    read = jnp.take(incoming, my_holder, axis=0, mode="clip").reshape(refs * NT, width)
    rows = lax.all_gather(read, "tensor", axis=0, tiled=False)
    pair_rows = project(rows, key_weight, value_weight)
    query_grad, pair, pair_t = attend_back(queries, out_grad, pair_rows, my_lengths)
    part = row_part(pair, key_weight, value_weight)
    row_grad = lax.psum_scatter(part, "tensor", scatter_dimension=1, tiled=True)
    key_weight_grad, value_weight_grad = weight_grads(pair_t, rows)
    returning = jnp.take(row_grad.reshape(refs, NT, width), back_ref, axis=0, mode="clip")
    arrived = lax.all_to_all(returning, "seq", split_axis=0, concat_axis=0, tiled=True)
    taken = jnp.take(arrived, slot_reader, axis=0, mode="clip")
    neighbour_grad = jnp.where(slot_live[:, None, None], taken, jnp.zeros((), BF16))
    return (
        query_grad,
        key_weight_grad,
        value_weight_grad,
        neighbour_grad.reshape(slot_count * NT, width),
    )


def solution(mesh):
    placed = (
        P("seq", "tensor"),
        P("seq", "tensor"),
        P("seq", "tensor"),
        P(None, "tensor"),
        P(None, "tensor"),
        P(),
        P(),
        P(),
    )
    return jax.shard_map(
        local,
        mesh=mesh,
        in_specs=placed,
        out_specs=(P("seq", "tensor"), P("seq", "tensor"), P("seq", "tensor"), P("seq", "tensor")),
        check_vma=False,
    )
```

time: 435 us -> 286 us (0.66)
  waiting for transfers between devices: 288 us -> 133 us
  matrix products: 66.7 us -> 0 us
  Pallas kernels: 0 us -> 57.2 us
  starting transfers between devices: 14.9 us -> 45.1 us
  local copies, waits for them, and re-layouts: 32.8 us -> 21 us
    reduce_scatter x2 -> x1, waiting for transfers between devices: 114 us -> 0.01 us  [local(): row_grad = lax.psum_scatter(part, 'tensor', scatter_dimension=1, tiled=True)]
    dot_general x11 -> x0, matrix products: 66.7 us -> none  [the longest x1 16.8 us: weight_term(): lax.dot_general(rows_here, grads_here, (((0,), (0,)), ((), ())), preferre...]
    all_to_all x1, waiting for transfers between devices: 58.8 us -> 0.01 us  [local(): lax.all_to_all(returning, 'seq', split_axis=0, concat_axis=0, tiled=True)]
    pallas_call x0 -> x6, Pallas kernels: none -> 57.2 us  [the longest x3 18.9 us: weight_groups(): pl.pallas_call(body, grid_spec=pltpu.PrefetchScalarGridSpec(num_scalar_pr...]
    ppermute x0 -> x24, waiting for transfers between devices: none -> 54.8 us  [shift(): return lax.ppermute(value, 'seq', [(i, moved(i)) for i in range(16)])]
    all_to_all x1, waiting for transfers between devices: 59.8 us -> 27.8 us  [local(): lax.all_to_all(outgoing, 'seq', split_axis=0, concat_axis=0, tiled=True)]
    ppermute x0 -> x24, starting transfers between devices: none -> 31.1 us  [shift(): return lax.ppermute(value, 'seq', [(i, moved(i)) for i in range(16)])]
    select_n x8 -> x1, other arithmetic: 10.5 us -> 2.5 us  [local(): jnp.where(slot_live[:, None, None], taken, jnp.zeros((), BF16))]
  transfers between devices with their start and end apart: 5 -> 28, of which waited for: 5 -> 9; matrix products, arithmetic and copies ran while one was open for 8% -> 9% of each run, Pallas kernels for 0% -> 7%
where the time goes in v1:
time: 286 us; the launch traced here: 285 us
  waiting for transfers between devices  133 us (47%)
  Pallas kernels  57.2 us (20%)
  starting transfers between devices  45.1 us (16%)
  local copies, waits for them, and re-layouts  21 us (7%)
  between operations  14.6 us (5%)
  other arithmetic  14.4 us (5%)
    ppermute x24, waiting for transfers between devices, shift(): return lax.ppermute(value, 'seq', [(i, moved(i)) for i in range(16)])  54.8 us
    all_gather x1, waiting for transfers between devices, local(): rows = lax.all_gather(read, 'tensor', axis=0, tiled=False)  50 us
    ppermute x24, starting transfers between devices, shift(): return lax.ppermute(value, 'seq', [(i, moved(i)) for i in range(16)])  31.1 us
    all_to_all x1, waiting for transfers between devices, local(): lax.all_to_all(outgoing, 'seq', split_axis=0, concat_axis=0, tiled=True)  27.8 us
    pallas_call x3, Pallas kernels, weight_groups(): pl.pallas_call(body, grid_spec=pltpu.PrefetchScalarGridSpec(num_scalar_pr...  18.9 us
    pallas_call x1, Pallas kernels, row_part(): pl.pallas_call(body, grid=(features // tile,), in_specs=[pl.BlockSpec((co...  14.4 us
    pallas_call x1, Pallas kernels, project(): pl.pallas_call(body, grid=(parts,), in_specs=[pl.BlockSpec((1, count, dep...  13 us
    pallas_call x1, Pallas kernels, attend_back(): pl.pallas_call(body, grid_spec=pltpu.PrefetchScalarGridSpec(num_scalar_pr...  10.9 us
  transfers between devices with their start and end apart: 28, of which 9 were waited for; matrix products, arithmetic and copies ran while one was open for 9% of the time, Pallas kernels for 7%

profile of v1, /device:TPU:6, one launch (start us, length us, event | category | flops | bytes accessed | tf_op | source)
XLA Modules:
  0.0 285.0 jit_solution(7643368430063712612)
XLA Ops:
  8.5 2.0 gather_fusion.1
  10.5 8.4 %all-to-all-start = ((bf16[16,128,512]{2,1,0:T(8,128)(2,1)}), bf16[16,128,512]{2,1,0:T(8,128)(2,1)S(1)}, u32[]{:S(2)}, u32[]{:S(2)}) async-start(bf16[16,128,512]{2,1,0:T(8,128)(2,1)} %gather_fusion.1), calls=%async_computation | async-start | bytes 4194304 | tf_op jit(solution)/shard_map/all_to_all | solution.py:287
  19.3 27.8 %all-to-all-done = bf16[16,128,512]{2,1,0:T(8,128)(2,1)S(1)} async-done(((bf16[16,128,512]{2,1,0:T(8,128)(2,1)}), bf16[16,128,512]{2,1,0:T(8,128)(2,1)S(1)}, u32[]{:S(2)}, u32[]{:S(2)}) %all-to-all-start) | async-done | bytes 2097184 | tf_op jit(solution)/shard_map/all_to_all | solution.py:287
  47.2 1.6 gather_fusion.2
  49.6 50.0 %all-gather.2.cloned.1.call-done.r_ref.refs_2_.refs_3_.refs_4_.refs_5_.refs_6_.refs_7_.refs_8_.refs_9_ = bf16[8,1024,512]{2,1,0:T(8,128)(2,1)} async-done(((bf16[1,1024,512]{2,1,0:T(8,128)(2,1)}), bf16[8,1024,512]{2,1,0:T(8,128)(2,1)}) %all-gather.2.cloned.1.call-update) | async-done | bytes 8388624 | tf_op jit(solution)/shard_map/all_gather | solution.py:289
  99.6 13.0 %project.1.kv_ref = bf16[1024,1024]{1,0:T(8,128)(2,1)S(1)} custom-call(bf16[8,1024,512]{2,1,0:T(8,128)(2,1)} %all-gather.2.cloned.1.call-done.r_ref.refs_2_.refs_3_.refs_4_.refs_5_.refs_6_.refs_7_.refs_8_.refs_9_, bf16[4096,512]{1,0:T(8,128)(2,1)} %k_ref.3, bf16[4096,512]{1,0:T(8,128)(2,1)} %v_ref.3), custom_call_target="tpu_custom_call" | custom-call | flops 8589934592 | bytes 20971520 | tf_op jit(solution)/shard_map/project/pallas_call | solution.py:47
  114.0 10.9 %attend_back.1 = (bf16[256,512]{1,0:T(8,128)(2,1)}, bf16[1024,1024]{1,0:T(8,128)(2,1)S(1)}, bf16[1024,1024]{1,0:T(8,128)(2,1)S(1)}) custom-call(s32[8]{0:T(128)S(1)} %gather_fusion, bf16[256,512]{1,0:T(8,128)(2,1)S(1)} %copy-done.5, bf16[256,512]{1,0:T(8,128)(2,1)S(1)} %copy-done.6, bf16[1024,1024]{1,0:T(8,128)(2,1)} %copy-done.4), custom_call_target="tpu_custom_call" | custom-call | flops 469762048 | bytes 8388608 | tf_op jit(solution)/shard_map/attend_back/pallas_call | solution.py:98
  124.9 14.4 %row_part.1 = bf16[1024,4096]{1,0:T(8,128)(2,1)} custom-call(bf16[1024,1024]{1,0:T(8,128)(2,1)S(1)} %get-tuple-element.41.p_ref, bf16[4096,512]{1,0:T(8,128)(2,1)} %k_ref.3, bf16[4096,512]{1,0:T(8,128)(2,1)} %v_ref.3), custom_call_target="tpu_custom_call" | custom-call | flops 8589934592 | bytes 18874368 | tf_op jit(solution)/shard_map/row_part/pallas_call | solution.py:169
  141.4 4.8 %weight_groups.5 = (bf16[2,512,256]{2,1,0:T(8,128)(2,1)S(1)}, bf16[2,512,256]{2,1,0:T(8,128)(2,1)S(1)}, bf16[2,512,256]{2,1,0:T(8,128)(2,1)S(1)}, bf16[2,512,256]{2,1,0:T(8,128)(2,1)S(1)}) custom-call(s32[16]{0:T(128)S(1)} %reshape.133.id_ref, bf16[1024,1024]{1,0:T(8,128)(2,1)S(1)} %get-tuple-element.24.refs_0_.refs_1_, ...), custom_call_target="tpu_custom_call" | custom-call | flops 2147483648 | bytes 6291456 | tf_op jit(solution)/shard_map/weight_groups/pallas_call | solution.py:141
  146.2 3.0 %collective-permute-start.16 = (bf16[2,512,256]{2,1,0:T(8,128)(2,1)S(1)}, bf16[2,512,256]{2,1,0:T(8,128)(2,1)S(1)}, u32[]{:S(2)}, u32[]{:S(2)}) collective-permute-start(bf16[2,512,256]{2,1,0:T(8,128)(2,1)S(1)} %get-tuple-element.40), channel_id=1, source_target_pairs={{0,96},{8,104},{16,112},{24,120},{32,0},{40,8},{48,16},{56,24},{64... | collective-permute-start | bytes 1572872 | tf_op jit(solution)/shard_map/ppermute | solution.py:190
  149.2 9.3 %weight_groups.4 = (bf16[2,512,256]{2,1,0:T(8,128)(2,1)S(1)}, bf16[2,512,256]{2,1,0:T(8,128)(2,1)S(1)}, bf16[2,512,256]{2,1,0:T(8,128)(2,1)S(1)}, bf16[2,512,256...) custom-call(s32[32]{0:T(128)S(1)} %reshape.132.id_ref, ...), custom_call_target="tpu_custom_call" | custom-call | flops 4294967296 | bytes 12582912 | tf_op jit(solution)/shard_map/weight_groups/pallas_call | solution.py:141
  158.6 3.2 %collective-permute-start.14 = (bf16[2,512,256]{2,1,0:T(8,128)(2,1)S(1)}, bf16[2,512,256]{2,1,0:T(8,128)(2,1)S(1)}, u32[]{:S(2)}, u32[]{:S(2)}) collective-permute-start(bf16[2,512,256]{2,1,0:T(8,128)(2,1)S(1)} %get-tuple-element.36), channel_id=1, source_target_pairs={{0,96},{8,104},{16,112},{24,120},{32,0},{40,8},{48,16},{56,24},{64... | collective-permute-start | bytes 1572872 | tf_op jit(solution)/shard_map/ppermute | solution.py:190
  162.6 4.8 %weight_groups.3 = (bf16[2,512,256]{2,1,0:T(8,128)(2,1)S(1)}, bf16[2,512,256]{2,1,0:T(8,128)(2,1)S(1)}, bf16[2,512,256]{2,1,0:T(8,128)(2,1)S(1)}, bf16[2,512,256]{2,1,0:T(8,128)(2,1)S(1)}) custom-call(s32[16]{0:T(128)S(1)} %reshape.131.id_ref, bf16[1024,1024]{1,0:T(8,128)(2,1)S(1)} %copy-done.3, bf16[1024,1024]{1,0:T(8,128)(2,1)S(1)} %copy-done.3, ...), custom_call_target="tpu_custom_call" | custom-call | flops 2147483648 | bytes 6291456 | tf_op jit(solution)/shard_map/weight_groups/pallas_call | solution.py:141
  167.4 2.6 collective-permute-start.3
  170.3 6.0 %collective-permute-done.4 = bf16[2,512,256]{2,1,0:T(8,128)(2,1)S(1)} collective-permute-done((bf16[2,512,256]{2,1,0:T(8,128)(2,1)S(1)}, bf16[2,512,256]{2,1,0:T(8,128)(2,1)S(1)}, u32[]{:S(2)}, u32[]{:S(2)}) %collective-permute-start.4) | collective-permute-done | bytes 524320 | tf_op jit(solution)/shard_map/ppermute | solution.py:190
  177.2 14.5 %collective-permute-done = bf16[2,512,256]{2,1,0:T(8,128)(2,1)S(1)} collective-permute-done((bf16[2,512,256]{2,1,0:T(8,128)(2,1)S(1)}, bf16[2,512,256]{2,1,0:T(8,128)(2,1)S(1)}, u32[]{:S(2)}, u32[]{:S(2)}) %collective-permute-start) | collective-permute-done | bytes 524320 | tf_op jit(solution)/shard_map/ppermute | solution.py:190
  195.8 1.8 collective-permute-start.1
  197.6 8.1 %collective-permute-done.13 = bf16[2,512,256]{2,1,0:T(8,128)(2,1)S(1)} collective-permute-done((bf16[2,512,256]{2,1,0:T(8,128)(2,1)S(1)}, bf16[2,512,256]{2,1,0:T(8,128)(2,1)S(1)}, u32[]{:S(2)}, u32[]{:S(2)}) %collective-permute-start.13) | collective-permute-done | bytes 524320 | tf_op jit(solution)/shard_map/ppermute | solution.py:190
  205.7 1.7 collective-permute-start.22
  209.8 8.6 %collective-permute-done.5 = bf16[2,512,256]{2,1,0:T(8,128)(2,1)S(1)} collective-permute-done((bf16[2,512,256]{2,1,0:T(8,128)(2,1)S(1)}, bf16[2,512,256]{2,1,0:T(8,128)(2,1)S(1)}, u32[]{:S(2)}, u32[]{:S(2)}) %collective-permute-start.5) | collective-permute-done | bytes 524320 | tf_op jit(solution)/shard_map/ppermute | solution.py:190
  220.0 3.2 %collective-permute-start.21 = (bf16[256,256]{1,0:T(8,128)(2,1)}, bf16[256,256]{1,0:T(8,128)(2,1)}, u32[]{:S(2)}, u32[]{:S(2)}) collective-permute-start(bf16[256,256]{1,0:T(8,128)(2,1)} %slice_bitcast_fusion.6), channel_id=1, source_target_pairs={{0,8},{8,16},{16,24},{24,0},{32,40},{40,48},{48,56},{56,32},{64,72... | collective-permute-start | bytes 393224 | tf_op jit(solution)/shard_map/ppermute | solution.py:190
  224.7 3.2 %gather_fusion.3 = bf16[16,128,512]{2,1,0:T(8,128)(2,1)} fusion(bf16[8,128,512]{2,1,0:T(8,128)(2,1)} %bitcast.129, s32[1024]{0:T(1024)S(1)} %pad_clamp_fusion.1), kind=kCustom, calls=%fused_computation.3 | custom fusion | bytes 4194368 | tf_op jit(solution)/shard_map/jit(_take)/gather | solution.py:295
  227.9 5.5 %all-to-all-start.1 = ((bf16[16,128,512]{2,1,0:T(8,128)(2,1)}), bf16[16,128,512]{2,1,0:T(8,128)(2,1)S(1)}, u32[]{:S(2)}, u32[]{:S(2)}) async-start(bf16[16,128,512]{2,1,0:T(8,128)(2,1)} %gather_fusion.3), calls=%async_computation.2 | async-start | bytes 4194304 | tf_op jit(solution)/shard_map/all_to_all | solution.py:296
  234.9 1.6 slice_bitcast_fusion.12
  239.0 1.8 collective-permute-start.8
  243.7 13.5 %collective-permute-done.6 = bf16[256,256]{1,0:T(8,128)(2,1)S(1)} collective-permute-done((bf16[256,256]{1,0:T(8,128)(2,1)}, bf16[256,256]{1,0:T(8,128)(2,1)S(1)}, u32[]{:S(2)}, u32[]{:S(2)}) %collective-permute-start.6) | collective-permute-done | bytes 131104 | tf_op jit(solution)/shard_map/ppermute | solution.py:190
  257.2 2.1 collective-permute-start.19
  260.4 3.2 %collective-permute-start.11 = (bf16[256,256]{1,0:T(8,128)(2,1)S(1)}, bf16[256,256]{1,0:T(8,128)(2,1)}, u32[]{:S(2)}, u32[]{:S(2)}) collective-permute-start(bf16[256,256]{1,0:T(8,128)(2,1)S(1)} %fusion.10), channel_id=1, source_target_pairs={{0,96},{8,104},{16,112},{24,120},{32,0},{40,8},{48,16},{56,24},{64... | collective-permute-start | bytes 393224 | tf_op jit(solution)/shard_map/ppermute | solution.py:190
  266.8 3.0 %collective-permute-done.7 = bf16[256,256]{1,0:T(8,128)(2,1)} collective-permute-done((bf16[256,256]{1,0:T(8,128)(2,1)S(1)}, bf16[256,256]{1,0:T(8,128)(2,1)}, u32[]{:S(2)}, u32[]{:S(2)}) %collective-permute-start.7) | collective-permute-done | bytes 131104 | tf_op jit(solution)/shard_map/ppermute | solution.py:190
  271.8 2.1 copy.28
  273.9 1.8 gather_fusion.4
  275.7 2.5 bitcast_select_fusion
  (119 shorter events, 30.3 us)
Async XLA Ops:
  10.5 36.7 %all-to-all-start = ((bf16[16,128,512]{2,1,0:T(8,128)(2,1)}), bf16[16,128,512]{2,1,0:T(8,128)(2,1)S(1)}, u32[]{:S(2)}, u32[]{:S(2)}) async-start(bf16[16,128,512]{2,1,0:T(8,128)(2,1)} %gather_fusion.1), calls=%async_computation | async-start | bytes 4194304 | tf_op jit(solution)/shard_map/all_to_all | solution.py:287
  18.9 29.9 %copy-start.8 = (s32[16,9]{1,0:T(8,128)S(1)}, s32[16,9]{1,0:T(8,128)}, u32[]{:S(2)}) copy-start(s32[16,9]{1,0:T(8,128)} %param.15) | copy-start | bytes 1732
  18.9 80.7 %all-gather.2.cloned.1.call-start = ((), (), s32[]{:S(2)}) async-start(), calls=%async_computation.3 | async-start | bytes 9437184 | tf_op jit(solution)/shard_map/all_gather | solution.py:289
  48.8 175.9 %reduce-scatter.2.cloned.1.call-start = ((), (), s32[]{:S(2)}) async-start(), calls=%async_computation.4 | async-start | bytes 9437184 | tf_op jit(solution)/shard_map/reduce_scatter | solution.py:293
  49.6 64.4 %copy-start.5 = (bf16[256,512]{1,0:T(8,128)(2,1)S(1)}, bf16[256,512]{1,0:T(8,128)(2,1)}, u32[]{:S(2)}) copy-start(bf16[256,512]{1,0:T(8,128)(2,1)} %q_ref.1) | copy-start | bytes 786436
  49.6 64.4 %copy-start.6 = (bf16[256,512]{1,0:T(8,128)(2,1)S(1)}, bf16[256,512]{1,0:T(8,128)(2,1)}, u32[]{:S(2)}) copy-start(bf16[256,512]{1,0:T(8,128)(2,1)} %g_ref.1) | copy-start | bytes 786436
  146.2 21.2 %collective-permute-start.16 = (bf16[2,512,256]{2,1,0:T(8,128)(2,1)S(1)}, bf16[2,512,256]{2,1,0:T(8,128)(2,1)S(1)}, u32[]{:S(2)}, u32[]{:S(2)}) collective-permute-start(bf16[2,512,256]{2,1,0:T(8,128)(2,1)S(1)} %get-tuple-element.40), channel_id=1, source_target_pairs={{0,96},{8,104},{16,112},{24,120},{32,0},{40,8},{48,16},{56,24},{64... | collective-permute-start | bytes 1572872 | tf_op jit(solution)/shard_map/ppermute | solution.py:190
  149.2 20.9 %collective-permute-start.12 = (bf16[2,512,256]{2,1,0:T(8,128)(2,1)S(1)}, bf16[2,512,256]{2,1,0:T(8,128)(2,1)S(1)}, u32[]{:S(2)}, u32[]{:S(2)}) collective-permute-start(bf16[2,512,256]{2,1,0:T(8,128)(2,1)S(1)} %get-tuple-element.35), channel_id=1, source_target_pairs={{0,32},{8,40},{16,48},{24,56},{32,64},{40,72},{48,80},{56,88},{64,... | collective-permute-start | bytes 1572872 | tf_op jit(solution)/shard_map/ppermute | solution.py:190
  158.6 34.0 %collective-permute-start.15 = (bf16[2,512,256]{2,1,0:T(8,128)(2,1)S(1)}, bf16[2,512,256]{2,1,0:T(8,128)(2,1)S(1)}, u32[]{:S(2)}, u32[]{:S(2)}) collective-permute-start(bf16[2,512,256]{2,1,0:T(8,128)(2,1)S(1)} %get-tuple-element.38), channel_id=1, source_target_pairs={{0,32},{8,40},{16,48},{24,56},{32,64},{40,72},{48,80},{56,88},{64,... | collective-permute-start | bytes 1572872 | tf_op jit(solution)/shard_map/ppermute | solution.py:190
  158.6 37.2 %collective-permute-start.14 = (bf16[2,512,256]{2,1,0:T(8,128)(2,1)S(1)}, bf16[2,512,256]{2,1,0:T(8,128)(2,1)S(1)}, u32[]{:S(2)}, u32[]{:S(2)}) collective-permute-start(bf16[2,512,256]{2,1,0:T(8,128)(2,1)S(1)} %get-tuple-element.36), channel_id=1, source_target_pairs={{0,96},{8,104},{16,112},{24,120},{32,0},{40,8},{48,16},{56,24},{64... | collective-permute-start | bytes 1572872 | tf_op jit(solution)/shard_map/ppermute | solution.py:190
  161.9 14.5 %collective-permute-start.4 = (bf16[2,512,256]{2,1,0:T(8,128)(2,1)S(1)}, bf16[2,512,256]{2,1,0:T(8,128)(2,1)S(1)}, u32[]{:S(2)}, u32[]{:S(2)}) collective-permute-start(bf16[2,512,256]{2,1,0:T(8,128)(2,1)S(1)} %get-tuple-element.32), channel_id=1, source_target_pairs={{0,24},{8,0},{16,8},{24,16},{32,56},{40,32},{48,40},{56,48},{64,88... | collective-permute-start | bytes 1572872 | tf_op jit(solution)/shard_map/ppermute | solution.py:190
  167.4 40.8 %collective-permute-start.3 = (bf16[2,512,256]{2,1,0:T(8,128)(2,1)S(1)}, bf16[2,512,256]{2,1,0:T(8,128)(2,1)S(1)}, u32[]{:S(2)}, u32[]{:S(2)}) collective-permute-start(bf16[2,512,256]{2,1,0:T(8,128)(2,1)S(1)} %get-tuple-element.30), channel_id=1, source_target_pairs={{0,8},{8,16},{16,24},{24,0},{32,40},{40,48},{48,56},{56,32},{64,72... | collective-permute-start | bytes 1572872 | tf_op jit(solution)/shard_map/ppermute | solution.py:190
  170.1 21.6 %collective-permute-start = (bf16[2,512,256]{2,1,0:T(8,128)(2,1)S(1)}, bf16[2,512,256]{2,1,0:T(8,128)(2,1)S(1)}, u32[]{:S(2)}, u32[]{:S(2)}) collective-permute-start(bf16[2,512,256]{2,1,0:T(8,128)(2,1)S(1)} %get-tuple-element.27), channel_id=1, source_target_pairs={{0,8},{8,16},{16,24},{24,0},{32,40},{40,48},{48,56},{56,32},{64,72... | collective-permute-start | bytes 1572872 | tf_op jit(solution)/shard_map/ppermute | solution.py:190
  176.3 16.3 %collective-permute-start.17 = (bf16[2,512,256]{2,1,0:T(8,128)(2,1)S(1)}, bf16[2,512,256]{2,1,0:T(8,128)(2,1)S(1)}, u32[]{:S(2)}, u32[]{:S(2)}) collective-permute-start(bf16[2,512,256]{2,1,0:T(8,128)(2,1)S(1)} %add_convert_fusion), channel_id=1, source_target_pairs={{0,96},{8,104},{16,112},{24,120},{32,0},{40,8},{48,16},{56,24},{64... | collective-permute-start | bytes 1572872 | tf_op jit(solution)/shard_map/ppermute | solution.py:190
  191.7 28.3 %collective-permute-start.2 = (bf16[2,512,256]{2,1,0:T(8,128)(2,1)S(1)}, bf16[2,512,256]{2,1,0:T(8,128)(2,1)S(1)}, u32[]{:S(2)}, u32[]{:S(2)}) collective-permute-start(bf16[2,512,256]{2,1,0:T(8,128)(2,1)S(1)} %get-tuple-element.28), channel_id=1, source_target_pairs={{0,24},{8,0},{16,8},{24,16},{32,56},{40,32},{48,40},{56,48},{64,88... | collective-permute-start | bytes 1572872 | tf_op jit(solution)/shard_map/ppermute | solution.py:190
  192.6 13.1 %collective-permute-start.13 = (bf16[2,512,256]{2,1,0:T(8,128)(2,1)S(1)}, bf16[2,512,256]{2,1,0:T(8,128)(2,1)S(1)}, u32[]{:S(2)}, u32[]{:S(2)}) collective-permute-start(bf16[2,512,256]{2,1,0:T(8,128)(2,1)S(1)} %add_convert_fusion.1), channel_id=1, source_target_pairs={{0,32},{8,40},{16,48},{24,56},{32,64},{40,72},{48,80},{56,88},{64,... | collective-permute-start | bytes 1572872 | tf_op jit(solution)/shard_map/ppermute | solution.py:190
  192.6 25.7 %collective-permute-start.5 = (bf16[2,512,256]{2,1,0:T(8,128)(2,1)S(1)}, bf16[2,512,256]{2,1,0:T(8,128)(2,1)S(1)}, u32[]{:S(2)}, u32[]{:S(2)}) collective-permute-start(bf16[2,512,256]{2,1,0:T(8,128)(2,1)S(1)} %add_convert_fusion.2), channel_id=1, source_target_pairs={{0,24},{8,0},{16,8},{24,16},{32,56},{40,32},{48,40},{56,48},{64,88... | collective-permute-start | bytes 1572872 | tf_op jit(solution)/shard_map/ppermute | solution.py:190
  194.4 29.4 %copy-start.7 = (bf16[1,512,256]{2,1,0:T(8,128)(2,1)}, bf16[1,512,256]{2,1,0:T(8,128)(2,1)S(1)}, u32[]{:S(2)}) copy-start(bf16[1,512,256]{2,1,0:T(8,128)(2,1)S(1)} %get-tuple-element.60) | copy-start | bytes 786436
  195.8 27.4 %collective-permute-start.1 = (bf16[2,512,256]{2,1,0:T(8,128)(2,1)S(1)}, bf16[2,512,256]{2,1,0:T(8,128)(2,1)S(1)}, u32[]{:S(2)}, u32[]{:S(2)}) collective-permute-start(bf16[2,512,256]{2,1,0:T(8,128)(2,1)S(1)} %add_convert_fusion.3), channel_id=1, source_target_pairs={{0,8},{8,16},{16,24},{24,0},{32,40},{40,48},{48,56},{56,32},{64,72... | collective-permute-start | bytes 1572872 | tf_op jit(solution)/shard_map/ppermute | solution.py:190
  205.7 30.8 %collective-permute-start.22 = (bf16[256,256]{1,0:T(8,128)(2,1)}, bf16[256,256]{1,0:T(8,128)(2,1)}, u32[]{:S(2)}, u32[]{:S(2)}) collective-permute-start(bf16[256,256]{1,0:T(8,128)(2,1)} %get-tuple-element.71), channel_id=1, source_target_pairs={{0,24},{8,0},{16,8},{24,16},{32,56},{40,32},{48,40},{56,48},{64,88... | collective-permute-start | bytes 393224 | tf_op jit(solution)/shard_map/ppermute | solution.py:190
  208.2 30.8 %collective-permute-start.18 = (bf16[256,256]{1,0:T(8,128)(2,1)}, bf16[256,256]{1,0:T(8,128)(2,1)}, u32[]{:S(2)}, u32[]{:S(2)}) collective-permute-start(bf16[256,256]{1,0:T(8,128)(2,1)} %get-tuple-element.70), channel_id=1, source_target_pairs={{0,8},{8,16},{16,24},{24,0},{32,40},{40,48},{48,56},{56,32},{64,72... | collective-permute-start | bytes 393224 | tf_op jit(solution)/shard_map/ppermute | solution.py:190
  218.4 41.9 %collective-permute-start.20 = (bf16[256,256]{1,0:T(8,128)(2,1)}, bf16[256,256]{1,0:T(8,128)(2,1)}, u32[]{:S(2)}, u32[]{:S(2)}) collective-permute-start(bf16[256,256]{1,0:T(8,128)(2,1)} %slice_bitcast_fusion.7), channel_id=1, source_target_pairs={{0,24},{8,0},{16,8},{24,16},{32,56},{40,32},{48,40},{56,48},{64,88... | collective-permute-start | bytes 393224 | tf_op jit(solution)/shard_map/ppermute | solution.py:190
  220.0 40.3 %collective-permute-start.21 = (bf16[256,256]{1,0:T(8,128)(2,1)}, bf16[256,256]{1,0:T(8,128)(2,1)}, u32[]{:S(2)}, u32[]{:S(2)}) collective-permute-start(bf16[256,256]{1,0:T(8,128)(2,1)} %slice_bitcast_fusion.6), channel_id=1, source_target_pairs={{0,8},{8,16},{16,24},{24,0},{32,40},{40,48},{48,56},{56,32},{64,72... | collective-permute-start | bytes 393224 | tf_op jit(solution)/shard_map/ppermute | solution.py:190
  223.3 18.5 %collective-permute-start.10 = (bf16[256,256]{1,0:T(8,128)(2,1)}, bf16[256,256]{1,0:T(8,128)(2,1)}, u32[]{:S(2)}, u32[]{:S(2)}) collective-permute-start(bf16[256,256]{1,0:T(8,128)(2,1)} %get-tuple-element.73), channel_id=1, source_target_pairs={{0,96},{8,104},{16,112},{24,120},{32,0},{40,8},{48,16},{56,24},{64... | collective-permute-start | bytes 393224 | tf_op jit(solution)/shard_map/ppermute | solution.py:190
  227.9 46.0 %all-to-all-start.1 = ((bf16[16,128,512]{2,1,0:T(8,128)(2,1)}), bf16[16,128,512]{2,1,0:T(8,128)(2,1)S(1)}, u32[]{:S(2)}, u32[]{:S(2)}) async-start(bf16[16,128,512]{2,1,0:T(8,128)(2,1)} %gather_fusion.3), calls=%async_computation.2 | async-start | bytes 4194304 | tf_op jit(solution)/shard_map/all_to_all | solution.py:296
  236.5 20.7 %collective-permute-start.6 = (bf16[256,256]{1,0:T(8,128)(2,1)}, bf16[256,256]{1,0:T(8,128)(2,1)S(1)}, u32[]{:S(2)}, u32[]{:S(2)}) collective-permute-start(bf16[256,256]{1,0:T(8,128)(2,1)} %get-tuple-element.72), channel_id=1, source_target_pairs={{0,32},{8,40},{16,48},{24,56},{32,64},{40,72},{48,80},{56,88},{64,... | collective-permute-start | bytes 393224 | tf_op jit(solution)/shard_map/ppermute | solution.py:190
  239.0 26.7 %collective-permute-start.8 = (bf16[256,256]{1,0:T(8,128)(2,1)}, bf16[256,256]{1,0:T(8,128)(2,1)S(1)}, u32[]{:S(2)}, u32[]{:S(2)}) collective-permute-start(bf16[256,256]{1,0:T(8,128)(2,1)} %slice_bitcast_fusion.13), channel_id=1, source_target_pairs={{0,96},{8,104},{16,112},{24,120},{32,0},{40,8},{48,16},{56,24},{64... | collective-permute-start | bytes 393224 | tf_op jit(solution)/shard_map/ppermute | solution.py:190
  241.8 21.8 %collective-permute-start.23 = (bf16[256,256]{1,0:T(8,128)(2,1)S(1)}, bf16[256,256]{1,0:T(8,128)(2,1)S(1)}, u32[]{:S(2)}, u32[]{:S(2)}) collective-permute-start(bf16[256,256]{1,0:T(8,128)(2,1)S(1)} %fusion.8), channel_id=1, source_target_pairs={{0,24},{8,0},{16,8},{24,16},{32,56},{40,32},{48,40},{56,48},{64,88... | collective-permute-start | bytes 393224 | tf_op jit(solution)/shard_map/ppermute | solution.py:190
  257.2 6.4 %collective-permute-start.19 = (bf16[256,256]{1,0:T(8,128)(2,1)S(1)}, bf16[256,256]{1,0:T(8,128)(2,1)S(1)}, u32[]{:S(2)}, u32[]{:S(2)}) collective-permute-start(bf16[256,256]{1,0:T(8,128)(2,1)S(1)} %fusion.9), channel_id=1, source_target_pairs={{0,8},{8,16},{16,24},{24,0},{32,40},{40,48},{48,56},{56,32},{64,72... | collective-permute-start | bytes 393224 | tf_op jit(solution)/shard_map/ppermute | solution.py:190
  260.3 6.6 %collective-permute-start.9 = (bf16[256,256]{1,0:T(8,128)(2,1)}, bf16[256,256]{1,0:T(8,128)(2,1)}, u32[]{:S(2)}, u32[]{:S(2)}) collective-permute-start(bf16[256,256]{1,0:T(8,128)(2,1)} %slice_bitcast_fusion.12), channel_id=1, source_target_pairs={{0,32},{8,40},{16,48},{24,56},{32,64},{40,72},{48,80},{56,88},{64,... | collective-permute-start | bytes 393224 | tf_op jit(solution)/shard_map/ppermute | solution.py:190
  260.4 6.5 %collective-permute-start.11 = (bf16[256,256]{1,0:T(8,128)(2,1)S(1)}, bf16[256,256]{1,0:T(8,128)(2,1)}, u32[]{:S(2)}, u32[]{:S(2)}) collective-permute-start(bf16[256,256]{1,0:T(8,128)(2,1)S(1)} %fusion.10), channel_id=1, source_target_pairs={{0,96},{8,104},{16,112},{24,120},{32,0},{40,8},{48,16},{56,24},{64... | collective-permute-start | bytes 393224 | tf_op jit(solution)/shard_map/ppermute | solution.py:190
  263.6 6.3 %collective-permute-start.7 = (bf16[256,256]{1,0:T(8,128)(2,1)S(1)}, bf16[256,256]{1,0:T(8,128)(2,1)}, u32[]{:S(2)}, u32[]{:S(2)}) collective-permute-start(bf16[256,256]{1,0:T(8,128)(2,1)S(1)} %fusion.11), channel_id=1, source_target_pairs={{0,32},{8,40},{16,48},{24,56},{32,64},{40,72},{48,80},{56,88},{64,... | collective-permute-start | bytes 393224 | tf_op jit(solution)/shard_map/ppermute | solution.py:190
  (7 other events, 56.0 us)
Sparse Core Ops, SparseCore 0:
  48.9 50.6 all-gather.1
  139.5 52.6 reduce-scatter.1
